TPU v7x, 128 devices: a whole 4x4x4 slice. The times are simulated.
128 devices in a mesh: dp: 2 (over x_lo), expert: 64 (over x_hi, z, y, core).
Axes of the slice: x: 4 (x_hi: 2, x_lo: 2; x = x_hi * 2 + x_lo), y: 4, z: 4, core: 2. Of those that a mesh axis runs over, the one named last changes fastest.
Arguments:
- tokens: bfloat16 [2048, 7168], P(('dp', 'expert')), may hold values from -6 to 6
- picks: int32 [2048, 8], P(('dp', 'expert')), may hold values from 0 to 63, all different within a row; in each aligned block of 16 rows (0 to 15, 16 to 31, ...) at most 4 rows name the same one
- mix_weights: float32 [2048, 8], P(('dp', 'expert')), may hold values from 0.1 to 0.6
- pairs: int32 [16, 2], replicated, may hold values from 0 to 63, as said below
- gate_weight: bfloat16 [64, 7168, 1024], P('expert', None, 'dp'), may hold values from -0.0625 to 0.0625
- up_weight: bfloat16 [64, 7168, 1024], P('expert', None, 'dp'), may hold values from -0.0625 to 0.0625
- down_weight: bfloat16 [64, 1024, 7168], P('expert', 'dp'), may hold values from -0.1875 to 0.1875
Outputs:
- combined: bfloat16 [2048, 7168], P(('dp', 'expert'))
Inputs may be any that keep to these rules, and one draw needn't show every extreme that they name: `picks`: each row names 8 different slots. The rows of one device name one slot at most 4 times, and in every draw some device's rows name some slot exactly 4 times. Each row is a pair (a, a + 32) with a below 32; no position stands in two pairs; positions 0 and 31 always stand in a pair.
All inputs are finite; a program needn't handle non-finite values.
Results may differ from a plain program's by a relative error of at most 0.012.
Values may be sent and summed in bfloat16 or wider, within the bound.
No kernel may reach another device: no remote copies, remote signals or barrier semaphores. Data moves between devices by JAX's collectives and lax.ppermute only.
A program may use at most 128 MiB of HBM per device.

v0:
```python
import jax
import jax.numpy as jnp
from jax import lax
from jax.sharding import PartitionSpec as P


def swapped(value, axis, distance):
    mask = 2**distance
    pairs = [(source, source ^ mask) for source in range(lax.axis_size(axis))]
    return lax.ppermute(value, axis, pairs)


def per_device(tokens, picks, mix_weights, pairs, gate_weight, up_weight, down_weight):
    experts = lax.axis_size("expert")
    own_index = lax.axis_index("expert")
    tok_rows, width = tokens.shape
    picks_each = picks.shape[1]
    capacity = max(4, tok_rows * picks_each * 2 // experts)
    slot_ids = jnp.arange(experts, dtype=jnp.int32)
    gate_w = gate_weight[0]
    up_w = up_weight[0]
    down_w = down_weight[0]
    top_bit = experts.bit_length() - 2
    partner_sets = swapped((gate_w, up_w, down_w), "expert", top_bit)
    moved = jnp.any(pairs == own_index)
    gate_w = jnp.where(moved, partner_sets[0], gate_w)
    up_w = jnp.where(moved, partner_sets[1], up_w)
    down_w = jnp.where(moved, partner_sets[2], down_w)
    flat_target = picks.reshape(-1)
    onehot = (flat_target[:, None] == slot_ids[None, :]).astype(jnp.int32)
    rank_run = jnp.cumsum(onehot, axis=0) - onehot
    position = jnp.sum(rank_run * onehot, axis=1)
    slot_index = flat_target * capacity + position
    repeated = jnp.repeat(tokens, picks_each, axis=0)
    buffer = jnp.zeros((experts * capacity, width), jnp.bfloat16).at[slot_index].set(repeated)
    buffer = buffer.reshape(experts, capacity, width)
    slab_rows = lax.all_gather(
        lax.all_to_all(buffer, "expert", split_axis=0, concat_axis=0, tiled=True),
        "dp",
        axis=0,
        tiled=True,
    )
    flat_rows = slab_rows.reshape(-1, width)
    gate_proj = jnp.dot(flat_rows, gate_w, preferred_element_type=jnp.float32)
    up_proj = jnp.dot(flat_rows, up_w, preferred_element_type=jnp.float32)
    hidden = (jax.nn.silu(gate_proj) * up_proj).astype(jnp.bfloat16)
    output = jnp.dot(hidden, down_w, preferred_element_type=jnp.float32)
    partial_value = output.reshape(slab_rows.shape[0], slab_rows.shape[1], width)
    own_sums = lax.psum_scatter(
        partial_value.astype(jnp.bfloat16), "dp", scatter_dimension=0, tiled=True
    )
    returned_rows = lax.all_to_all(own_sums, "expert", split_axis=0, concat_axis=0, tiled=True)
    picked = returned_rows.reshape(experts * capacity, width)[slot_index]
    picked = picked.reshape(tok_rows, picks_each, width).astype(jnp.float32)
    mixed = jnp.einsum("tkd,tk->td", picked, mix_weights)
    return mixed.astype(jnp.bfloat16)


def solution(mesh):
    return jax.shard_map(
        per_device,
        mesh=mesh,
        in_specs=(
            P(("dp", "expert"), None),
            P(("dp", "expert"), None),
            P(("dp", "expert"), None),
            P(),
            P("expert", None, "dp"),
            P("expert", None, "dp"),
            P("expert", "dp", None),
        ),
        out_specs=P(("dp", "expert"), None),
        check_vma=False,
    )
```

profile of v0, /device:TPU:1, one launch (start us, length us, event | category | flops | bytes accessed | tf_op | source)
XLA Modules:
  0.0 923.8 jit_solution(8518033084992864062)
XLA Ops:
  6.5 0.0 copy-start
  6.5 0.0 all-gather.2.cloned.1.call-start
  6.5 0.8 copy.13
  7.3 0.7 broadcast_multiply_fusion
  8.0 0.1 eq.21
  8.1 0.1 fusion.15
  8.2 0.2 reduce_window_sum.11
  8.4 0.2 select_reduce_fusion
  8.6 0.1 copy.12
  8.6 0.1 mul.28
  8.7 0.0 copy-done
  8.8 5.4 scatter_custom_fusion
  14.2 7.0 reshape.48
  21.1 0.0 copy-start.4
  21.1 58.7 %all_to_all.10 = bf16[64,4,7168]{2,1,0:T(4,128)(2,1)} all-to-all(bf16[64,4,7168]{2,1,0:T(4,128)(2,1)} %reshape.48), channel_id=1, replica_groups=mesh['dp'=2,'expert'=64] {'expert'}, dimensions={0} | all-to-all | bytes 7340032 | tf_op jit(solution)/shard_map/all_to_all | solution.py:38
  79.8 0.0 all-gather.2.cloned.1.call-update
  79.9 0.0 all-reduce.3.cloned.1.call-start
  79.9 1.6 collective-permute-start.1
  81.5 1.4 collective-permute-start
  83.0 1.5 collective-permute-start.2
  84.5 0.0 copy-done.4
  84.5 0.6 compare_reduce_fusion
  85.1 168.9 %all-gather.2.cloned.1.call-done = bf16[128,4,7168]{2,1,0:T(4,128)(2,1)} async-done(((bf16[64,4,7168]{2,1,0:T(4,128)(2,1)}), bf16[128,4,7168]{2,1,0:T(4,128)(2,1)}) %all-gather.2.cloned.1.call-update) | async-done | bytes 7340048 | tf_op jit(solution)/shard_map/all_gather | solution.py:37
  254.0 12.1 %reshape.49 = bf16[512,7168]{1,0:T(8,128)(2,1)} reshape(bf16[128,4,7168]{2,1,0:T(4,128)(2,1)} %all-gather.2.cloned.1.call-done) | data formatting | bytes 14680064 | tf_op jit(solution)/shard_map/reshape | solution.py:43
  266.1 0.0 copy-start.2
  266.1 53.5 %collective-permute-done.1 = bf16[7168,512]{1,0:T(8,128)(2,1)} collective-permute-done((bf16[7168,512]{1,0:T(8,128)(2,1)}, bf16[7168,512]{1,0:T(8,128)(2,1)}, u32[]{:S(2)}, u32[]{:S(2)}) %collective-permute-start.1) | collective-permute-done | bytes 7340064 | tf_op jit(solution)/shard_map/ppermute | solution.py:10
  319.6 9.1 fusion.1
  328.8 148.1 %collective-permute-done = bf16[7168,512]{1,0:T(8,128)(2,1)} collective-permute-done((bf16[7168,512]{1,0:T(8,128)(2,1)}, bf16[7168,512]{1,0:T(8,128)(2,1)}, u32[]{:S(2)}, u32[]{:S(2)}) %collective-permute-start) | collective-permute-done | bytes 7340064 | tf_op jit(solution)/shard_map/ppermute | solution.py:10
  476.9 0.0 copy-done.2
  476.9 7.3 fusion.3
  484.2 150.0 %collective-permute-done.2 = bf16[512,7168]{1,0:T(8,128)(2,1)} collective-permute-done((bf16[512,7168]{1,0:T(8,128)(2,1)}, bf16[512,7168]{1,0:T(8,128)(2,1)}, u32[]{:S(2)}, u32[]{:S(2)}) %collective-permute-start.2) | collective-permute-done | bytes 7340064 | tf_op jit(solution)/shard_map/ppermute | solution.py:10
  634.2 9.9 %convolution_convert_fusion = bf16[512,7168]{1,0:T(8,128)(2,1)} fusion(bf16[512,7168]{1,0:T(8,128)(2,1)} %collective-permute-done.2, pred[]{:T(512)} %compare_reduce_fusion, f32[512,512]{1,0:T(8,128)S(1)} %fusion.1, f32[512,512]{1,0:T(8,128)S(1)} %fusion.3, bf16[1,512,7168]{2,1,0:T(8,128)(2,1)} %param.13), kind=kOutput, calls=%fused_computation.2 | convolution fusion | flops 3767009280 | bytes 24117248 | tf_op jit(solution)/shard_map/dot_general | solution.py:47
  644.2 12.7 %convert_element_type.19 = bf16[128,4,7168]{2,1,0:T(4,128)(2,1)} reshape(bf16[512,7168]{1,0:T(8,128)(2,1)} %convolution_convert_fusion) | data formatting | bytes 14680064 | tf_op jit(solution)/shard_map/convert_element_type | solution.py:50
  656.8 0.0 all-reduce.3.cloned.1.call-update
  656.9 0.6 copy-done.5
  657.5 0.6 dynamic-slice
  658.7 0.0 copy-start.3
  658.7 182.9 %all-reduce.3.cloned.1.call-done = bf16[128,4,7168]{2,1,0:T(4,128)(2,1)} async-done(((bf16[128,4,7168]{2,1,0:T(4,128)(2,1)}), bf16[128,4,7168]{2,1,0:T(4,128)(2,1)}) %all-reduce.3.cloned.1.call-update) | async-done | bytes 7340048
  841.7 5.2 constant_dynamic-slice_fusion
  846.9 10.4 %all-to-all-start.1 = ((bf16[64,4,7168]{2,1,0:T(4,128)(2,1)}), bf16[64,4,7168]{2,1,0:T(4,128)(2,1)}, u32[]{:S(2)}, u32[]{:S(2)}) async-start(bf16[64,4,7168]{2,1,0:T(4,128)(2,1)} %constant_dynamic-slice_fusion), calls=%async_computation.1 | async-start | bytes 7340032 | tf_op jit(solution)/shard_map/all_to_all | solution.py:52
  857.3 0.0 copy-done.3
  857.3 0.1 copy.14
  857.4 45.5 %all-to-all-done.1 = bf16[64,4,7168]{2,1,0:T(4,128)(2,1)} async-done(((bf16[64,4,7168]{2,1,0:T(4,128)(2,1)}), bf16[64,4,7168]{2,1,0:T(4,128)(2,1)}, u32[]{:S(2)}, u32[]{:S(2)}) %all-to-all-start.1) | async-done | bytes 3670048 | tf_op jit(solution)/shard_map/all_to_all | solution.py:52
  902.9 6.8 reshape.50
  909.7 5.9 gather_fusion
  915.5 0.6 fusion.8
  916.2 0.8 copy.17
  916.9 0.0 copy-done.1
  (4 shorter events, 0.0 us)
Async XLA Ops:
  6.5 2.2 copy-start
  6.5 247.5 %all-gather.2.cloned.1.call-start = ((), (), s32[]{:S(2)}) async-start(), calls=%async_computation.2 | async-start | bytes 11010048 | tf_op jit(solution)/shard_map/all_gather | solution.py:37
  21.1 63.4 %copy-start.4 = (s32[16,2]{0,1:T(2,128)S(1)}, s32[16,2]{0,1:T(2,128)}, u32[]{:S(2)}) copy-start(s32[16,2]{0,1:T(2,128)} %param.10) | copy-start | bytes 388
  79.9 761.8 %all-reduce.3.cloned.1.call-start = ((), (), s32[]{:S(2)}) async-start(), calls=%async_computation.3 | async-start | bytes 14680064
  79.9 239.7 %collective-permute-start.1 = (bf16[7168,512]{1,0:T(8,128)(2,1)}, bf16[7168,512]{1,0:T(8,128)(2,1)}, u32[]{:S(2)}, u32[]{:S(2)}) collective-permute-start(bf16[7168,512]{1,0:T(8,128)(2,1)} %bitcast.36), channel_id=1, source_target_pairs={{0,32},{1,33},{2,34},{3,35},{4,36},{5,37},{6,38},{7,39},{8,40},{9,... | collective-permute-start | bytes 22020104 | tf_op jit(solution)/shard_map/ppermute | solution.py:10
  81.5 395.4 %collective-permute-start = (bf16[7168,512]{1,0:T(8,128)(2,1)}, bf16[7168,512]{1,0:T(8,128)(2,1)}, u32[]{:S(2)}, u32[]{:S(2)}) collective-permute-start(bf16[7168,512]{1,0:T(8,128)(2,1)} %bitcast.37), channel_id=1, source_target_pairs={{0,32},{1,33},{2,34},{3,35},{4,36},{5,37},{6,38},{7,39},{8,40},{9,... | collective-permute-start | bytes 22020104 | tf_op jit(solution)/shard_map/ppermute | solution.py:10
  83.0 551.3 %collective-permute-start.2 = (bf16[512,7168]{1,0:T(8,128)(2,1)}, bf16[512,7168]{1,0:T(8,128)(2,1)}, u32[]{:S(2)}, u32[]{:S(2)}) collective-permute-start(bf16[512,7168]{1,0:T(8,128)(2,1)} %bitcast.38), channel_id=1, source_target_pairs={{0,32},{1,33},{2,34},{3,35},{4,36},{5,37},{6,38},{7,39},{8,40},{9,... | collective-permute-start | bytes 22020104 | tf_op jit(solution)/shard_map/ppermute | solution.py:10
  266.1 210.8 %copy-start.2 = (bf16[512,7168]{1,0:T(8,128)(2,1)S(1)}, bf16[512,7168]{1,0:T(8,128)(2,1)}, u32[]{:S(2)}) copy-start(bf16[512,7168]{1,0:T(8,128)(2,1)} %reshape.49) | copy-start | bytes 22020100
  656.8 0.7 copy-start.5
  658.7 198.5 %copy-start.3 = (f32[16,8]{0,1:T(8,128)S(1)}, f32[16,8]{0,1:T(8,128)}, u32[]{:S(2)}) copy-start(f32[16,8]{0,1:T(8,128)} %param.9) | copy-start | bytes 1540
  846.9 56.0 %all-to-all-start.1 = ((bf16[64,4,7168]{2,1,0:T(4,128)(2,1)}), bf16[64,4,7168]{2,1,0:T(4,128)(2,1)}, u32[]{:S(2)}, u32[]{:S(2)}) async-start(bf16[64,4,7168]{2,1,0:T(4,128)(2,1)} %constant_dynamic-slice_fusion), calls=%async_computation.1 | async-start | bytes 7340032 | tf_op jit(solution)/shard_map/all_to_all | solution.py:52
  902.9 14.1 %copy-start.1 = (bf16[16,7168]{1,0:T(8,128)(2,1)S(1)}, bf16[16,7168]{1,0:T(8,128)(2,1)}, u32[]{:S(2)}) copy-start(bf16[16,7168]{1,0:T(8,128)(2,1)} %param.7) | copy-start | bytes 688132
Sparse Core Ops, SparseCore 0:
  80.0 174.0 all-gather.1
  657.0 184.6 all-reduce.2
where the time goes:
time: 929 us; the launch traced here: 924 us
  waiting for transfers between devices  749 us (81%)
  blocking collectives  58.7 us (6%)
  local copies, waits for them, and re-layouts  58.1 us (6%)
  matrix products  27 us (3%)
  starting transfers between devices  15 us (2%)
  between operations  14.2 us (2%)
    ppermute x3, waiting for transfers between devices, swapped(): return lax.ppermute(value, axis, pairs)  352 us
    unnamed x3, waiting for transfers between devices  183 us
    all_gather x1, waiting for transfers between devices, per_device(): lax.all_gather(lax.all_to_all(buffer, 'expert', split_axis=0, concat_axis...  169 us
    all_to_all x1, blocking collectives, per_device(): lax.all_to_all(buffer, 'expert', split_axis=0, concat_axis=0, tiled=True)  58.7 us
    all_to_all x1, waiting for transfers between devices, per_device(): lax.all_to_all(own_sums, 'expert', split_axis=0, concat_axis=0, tiled=True)  45.5 us
  transfers between devices with their start and end apart: 6, of which 6 were waited for; matrix products, arithmetic and copies ran while one was open for 3% of the time, Pallas kernels for 0%

commit v1 on v0

v1 whole, which is shorter than its diff:
```python
import jax
import jax.numpy as jnp
from jax import lax
from jax.sharding import Mesh, PartitionSpec as P

X_AXES = ("dp", "xh")
ZY_AXES = ("z", "y")
ALL_AXES = ("dp", "xh", "z", "y", "c")
META = 128


def other_core(value):
    return lax.ppermute(value, "c", [(0, 1), (1, 0)])


def per_device(tokens, picks, mix_weights, pairs, gate_weight, up_weight, down_weight):
    tok_rows, width = tokens.shape
    top = picks.shape[1]
    xs = lax.axis_size("dp") * lax.axis_size("xh")
    columns = lax.axis_size("z") * lax.axis_size("y")
    cores = lax.axis_size("c")
    half = lax.axis_size("xh") * columns * cores // 2
    cap = 4
    groups = cores * xs
    pooled = groups * tok_rows
    rows = columns * groups * cap

    moved = jnp.any(picks[:, :, None] == pairs.reshape(-1), axis=-1)
    owner = jnp.where(moved, picks ^ half, picks)

    mix_hi = lax.reduce_precision(mix_weights, 8, 7)
    mix_lo = mix_weights - mix_hi
    meta = jnp.concatenate([owner.astype(jnp.float32), mix_hi, mix_lo], axis=1)
    meta = jnp.pad(meta, ((0, 0), (0, META - 3 * top))).astype(jnp.bfloat16)
    packed = jnp.concatenate([tokens, meta], axis=1)
    line = lax.all_gather(packed, X_AXES, axis=0, tiled=True)
    line = jnp.concatenate([line, other_core(line)], axis=0)
    pool = line[:, :width]
    meta = line[:, width:].astype(jnp.float32)
    owner = meta[:, :top].astype(jnp.int32)
    mix_hi = meta[:, top:2 * top]
    mix_lo = meta[:, 2 * top:3 * top]

    own_xh = lax.axis_index("xh")
    own_c = lax.axis_index("c")
    column_owner = own_xh * half + jnp.arange(columns, dtype=jnp.int32) * cores + own_c
    match = owner[None, :, :] == column_owner[:, None, None]
    hit = jnp.any(match, axis=2)
    hi = jnp.sum(jnp.where(match, mix_hi[None], 0.0), axis=2)
    lo = jnp.sum(jnp.where(match, mix_lo[None], 0.0), axis=2)
    counts = hit.astype(jnp.int32).reshape(columns, groups, tok_rows)
    rank = (jnp.cumsum(counts, axis=2) - counts).reshape(columns, pooled)
    slot_group = jnp.arange(groups * cap, dtype=jnp.int32) // cap
    slot_rank = jnp.arange(groups * cap, dtype=jnp.int32) % cap
    token_group = jnp.arange(pooled, dtype=jnp.int32) // tok_rows
    place = (
        hit[:, None, :]
        & (rank[:, None, :] == slot_rank[None, :, None])
        & (slot_group[None, :, None] == token_group[None, None, :])
    )
    spread = place.astype(jnp.bfloat16).reshape(rows, pooled)
    weight_hi = jnp.where(place, hi[:, None, :], 0.0).astype(jnp.bfloat16).reshape(rows, pooled)
    weight_lo = jnp.where(place, lo[:, None, :], 0.0).astype(jnp.bfloat16).reshape(rows, pooled)

    send = jnp.dot(spread, pool, preferred_element_type=jnp.float32).astype(jnp.bfloat16)
    recv = lax.all_to_all(send, ZY_AXES, split_axis=0, concat_axis=0, tiled=True)

    gate = jnp.dot(recv, gate_weight[0], preferred_element_type=jnp.float32)
    up = jnp.dot(recv, up_weight[0], preferred_element_type=jnp.float32)
    hidden = (jax.nn.silu(gate) * up).astype(jnp.bfloat16)
    output = jnp.dot(hidden, down_weight[0], preferred_element_type=jnp.float32).astype(jnp.bfloat16)

    back = lax.all_to_all(output, ZY_AXES, split_axis=0, concat_axis=0, tiled=True)
    mixer = jnp.concatenate([weight_hi, weight_lo], axis=1)
    mixed = lax.dot_general(mixer, back, (((0,), (0,)), ((), ())), preferred_element_type=jnp.float32)
    mixed = mixed[:pooled] + mixed[pooled:]
    near = mixed[:pooled // 2]
    far = other_core(mixed[pooled // 2:].astype(jnp.bfloat16))
    part = (near + far.astype(jnp.float32)).astype(jnp.bfloat16)
    parts = lax.all_to_all(part, X_AXES, split_axis=0, concat_axis=0, tiled=True)
    parts = parts.reshape(xs, tok_rows, width).astype(jnp.float32)
    return jnp.sum(parts, axis=0).astype(jnp.bfloat16)


def solution(mesh):
    fine = Mesh(mesh.devices.reshape(2, 2, 4, 4, 2), ALL_AXES)
    expert = ("xh", "z", "y", "c")
    return jax.shard_map(
        per_device,
        mesh=fine,
        in_specs=(
            P(ALL_AXES, None),
            P(ALL_AXES, None),
            P(ALL_AXES, None),
            P(),
            P(expert, None, "dp"),
            P(expert, None, "dp"),
            P(expert, "dp", None),
        ),
        out_specs=P(ALL_AXES, None),
        check_vma=False,
    )
```

time: 929 us -> 289 us (0.31)
  waiting for transfers between devices: 749 us -> 109 us
  blocking collectives: 58.7 us -> 130 us
  local copies, waits for them, and re-layouts: 58.1 us -> 6.15 us
  between operations: 14.2 us -> 0.18 us
    ppermute x3 -> x2, waiting for transfers between devices: 352 us -> 2.82 us  [other_core(): return lax.ppermute(value, 'c', [(0, 1), (1, 0)])]
    unnamed x3 -> x0, waiting for transfers between devices: 183 us -> none
    all_gather x1 -> x0, waiting for transfers between devices: 169 us -> none  [per_device(): lax.all_gather(lax.all_to_all(buffer, 'expert', split_axis=0, concat_axis...]
    all_to_all x1, waiting for transfers between devices: 45.5 us -> 106 us  [per_device(): lax.all_to_all(output, ZY_AXES, split_axis=0, concat_axis=0, tiled=True)]
    all_to_all x1 -> x2, blocking collectives: 58.7 us -> 108 us  [the longest x1 91.6 us: per_device(): lax.all_to_all(send, ZY_AXES, split_axis=0, concat_axis=0, tiled=True)]
    reshape x3 -> x0, local copies, waits for them, and re-layouts: 25.9 us -> none  [the longest x1 12.1 us: per_device(): flat_rows = slab_rows.reshape(-1, width)]
    all_gather x0 -> x1, blocking collectives: none -> 21.9 us  [per_device(): line = lax.all_gather(packed, X_AXES, axis=0, tiled=True)]
    convert_element_type x1, local copies, waits for them, and re-layouts: 12.7 us -> 0.08 us  [per_device(): counts = hit.astype(jnp.int32).reshape(columns, groups, tok_rows)]
  transfers between devices with their start and end apart: 6 -> 3, of which waited for: 6 -> 3; matrix products, arithmetic and copies ran while one was open for 3% -> 1% of each run, Pallas kernels for 0% -> 0%
where the time goes in v1:
time: 289 us; the launch traced here: 288 us
  blocking collectives  130 us (45%)
  waiting for transfers between devices  109 us (38%)
  matrix products  26.3 us (9%)
  other arithmetic  8.31 us (3%)
  starting transfers between devices  8.29 us (3%)
  local copies, waits for them, and re-layouts  6.15 us (2%)
    all_to_all x1, waiting for transfers between devices, per_device(): lax.all_to_all(output, ZY_AXES, split_axis=0, concat_axis=0, tiled=True)  106 us
    all_to_all x1, blocking collectives, per_device(): lax.all_to_all(send, ZY_AXES, split_axis=0, concat_axis=0, tiled=True)  91.6 us
    all_gather x1, blocking collectives, per_device(): line = lax.all_gather(packed, X_AXES, axis=0, tiled=True)  21.9 us
    all_to_all x1, blocking collectives, per_device(): lax.all_to_all(part, X_AXES, split_axis=0, concat_axis=0, tiled=True)  16.6 us
    dot_general x1, matrix products, per_device(): jnp.dot(hidden, down_weight[0], preferred_element_type=jnp.float32)  9.19 us
  transfers between devices with their start and end apart: 3, of which 3 were waited for; matrix products, arithmetic and copies ran while one was open for 1% of the time, Pallas kernels for 0%

profile of v1, /device:TPU:1, one launch (start us, length us, event | category | flops | bytes accessed | tf_op | source)
XLA Modules:
  0.0 288.0 jit_solution(644994550385983189)
XLA Ops:
  0.0 0.7 reduce-precision_convert_fusion
  0.7 0.8 copy.28
  1.4 0.1 eq.71
  1.5 0.8 copy.27
  2.3 0.4 compare_reduce_fusion.1
  2.7 0.1 copy.29
  2.8 0.7 fusion.27
  3.5 0.1 copy.33
  3.6 1.0 fusion.22
  4.6 21.9 %all_gather.3 = bf16[64,7296]{1,0:T(8,128)(2,1)S(1)} all-gather(bf16[16,7296]{1,0:T(8,128)(2,1)S(1)} %fusion.22), channel_id=1, replica_groups=mesh['dp'=2,'xh'=2,'z'=4,'y'=4,'c'=2] {'dp','xh'}, dimensions={0}, use_global_device_ids=true | all-gather | bytes 1167360 | tf_op jit(solution)/shard_map/all_gather | solution.py:36
  26.5 0.7 collective-permute-start
  27.2 1.3 copy.31
  28.6 0.1 eq.80
  28.7 0.1 broadcast_compare_fusion
  28.7 0.7 collective-permute-done
  29.5 2.7 copy.32
  32.1 0.8 fusion.28
  32.9 0.1 compare_reduce_fusion
  33.0 0.1 reshape.118
  33.1 2.7 reduce_window_sum.13
  35.8 0.1 reduce_window_sum.14
  35.9 0.1 fusion.21
  36.0 0.0 slice-start
  36.0 3.8 %convolution_convert_fusion.1 = bf16[512,7168]{1,0:T(8,128)(2,1)S(1)} fusion(pred[512,128]{1,0:T(32,128)(4,1)S(1)} %fusion.21, bf16[64,7296]{0,1:T(8,128)(2,1)} %copy.32, bf16[64,7296]{0,1:T(8,128)(2,1)S(1)} %copy.31), kind=kOutput, calls=%fused_computation.1 | convolution fusion | flops 946864128 | bytes 9273344 | tf_op jit(solution)/shard_map/dot_general | solution.py:65
  39.9 0.0 slice-start.1
  39.9 0.0 slice-start.2
  39.9 91.6 %all_to_all.33 = bf16[16,32,7168]{2,1,0:T(8,128)(2,1)S(1)} all-to-all(bf16[16,32,7168]{2,1,0:T(8,128)(2,1)S(1)} %bitcast.53), channel_id=1, replica_groups=mesh['dp'=2,'xh'=2,'z'=4,'y'=4,'c'=2] {'z','y'}, dimensions={0} | all-to-all | bytes 14680064 | tf_op jit(solution)/shard_map/all_to_all | solution.py:66
  131.5 0.0 slice-done
  131.5 0.0 slice-done.1
  131.5 0.0 slice-start.3
  131.5 3.9 %fusion.3 = f32[512,512]{1,0:T(8,128)S(1)} fusion(bf16[512,7168]{1,0:T(8,128)(2,1)S(1)} %bitcast.55, bf16[1,7168,512]{2,1,0:T(8,128)(2,1)S(1)} %bitcast.59), kind=kOutput, calls=%fused_computation.5 | convolution fusion | flops 3758096384 | bytes 15728640 | tf_op jit(solution)/shard_map/dot_general | solution.py:68
  135.4 0.0 slice-done.2
  135.5 0.0 slice-done.3
  135.5 4.0 %fusion.10 = bf16[512,512]{1,0:T(8,128)(2,1)S(1)} fusion(bf16[512,7168]{1,0:T(8,128)(2,1)S(1)} %bitcast.56, bf16[1,7168,512]{2,1,0:T(8,128)(2,1)S(1)} %bitcast.61, f32[512,512]{1,0:T(8,128)S(1)} %fusion.3), kind=kOutput, calls=%fused_computation.14 | convolution fusion | flops 3759669248 | bytes 16252928 | tf_op jit(solution)/shard_map/dot_general | solution.py:69
  139.5 9.2 %convolution_convert_fusion = bf16[512,7168]{1,0:T(8,128)(2,1)} fusion(bf16[512,512]{1,0:T(8,128)(2,1)S(1)} %fusion.10, bf16[1,512,7168]{2,1,0:T(8,128)(2,1)} %param.13), kind=kOutput, calls=%fused_computation | convolution fusion | flops 3761766400 | bytes 15204352 | tf_op jit(solution)/shard_map/dot_general | solution.py:71
  148.7 4.9 %all-to-all-start.1 = ((bf16[16,32,7168]{2,1,0:T(8,128)(2,1)}), bf16[16,32,7168]{2,1,0:T(8,128)(2,1)}, u32[]{:S(2)}, u32[]{:S(2)}) async-start(bf16[16,32,7168]{2,1,0:T(8,128)(2,1)} %bitcast.54), calls=%async_computation.1 | async-start | bytes 14680064 | tf_op jit(solution)/shard_map/all_to_all | solution.py:73
  153.6 0.1 fusion.23
  153.7 0.1 fusion.19
  153.8 105.9 %all-to-all-done.1 = bf16[16,32,7168]{2,1,0:T(8,128)(2,1)} async-done(((bf16[16,32,7168]{2,1,0:T(8,128)(2,1)}), bf16[16,32,7168]{2,1,0:T(8,128)(2,1)}, u32[]{:S(2)}, u32[]{:S(2)}) %all-to-all-start.1) | async-done | bytes 7340064 | tf_op jit(solution)/shard_map/all_to_all | solution.py:73
  259.7 5.3 %fusion.14 = f32[256,7168]{1,0:T(8,128)S(1)} fusion(bf16[512,7168]{1,0:T(8,128)(2,1)} %bitcast.11, bf16[512,128]{1,0:T(8,128)(2,1)S(1)} %get-tuple-element.11, bf16[512,128]{1,0:T(8,128)(2,1)S(1)} %get-tuple-element.10), kind=kOutput, calls=%fused_computation.17 | convolution fusion | flops 1879572480 | bytes 14942208 | tf_op jit(solution)/shard_map/dot_general | solution.py:75
  265.0 0.4 slice_add_fusion
  265.5 0.1 slice.47
  265.6 2.7 collective-permute-start.1
  268.3 2.1 collective-permute-done.1
  270.4 0.2 fusion.5
  270.5 16.6 %all_to_all.34 = bf16[4,16,7168]{2,1,0:T(8,128)(2,1)S(1)} all-to-all(bf16[4,16,7168]{2,1,0:T(8,128)(2,1)S(1)} %bitcast.57), channel_id=1, replica_groups=mesh['dp'=2,'xh'=2,'z'=4,'y'=4,'c'=2] {'dp','xh'}, dimensions={0} | all-to-all | bytes 1835008 | tf_op jit(solution)/shard_map/all_to_all | solution.py:80
  287.1 0.9 reduce_sum.32
  (10 shorter events, 0.0 us)
Async XLA Ops:
  26.5 3.0 %collective-permute-start = (bf16[64,7296]{1,0:T(8,128)(2,1)S(1)}, bf16[64,7296]{1,0:T(8,128)(2,1)}, u32[]{:S(2)}, u32[]{:S(2)}) collective-permute-start(bf16[64,7296]{1,0:T(8,128)(2,1)S(1)} %all_gather.3), channel_id=1, source_target_pairs={{0,1},{1,0},{2,3},{3,2},{4,5},{5,4},{6,7},{7,6},{8,9},{9,8},{10,11... | collective-permute-start | bytes 2801672 | tf_op jit(solution)/shard_map/ppermute | solution.py:13
  36.0 95.5 %slice-start = ((s8[7340032]{0:T(1024)(128)(4,1)}), s8[3145728]{0:T(1024)(128)(4,1)S(1)}, s32[]{:S(2)}) async-start(s8[7340032]{0:T(1024)(128)(4,1)} %bitcast.58), calls=%async_computation.3 | async-start | bytes 6291456
  39.9 91.6 %slice-start.1 = ((s8[7340032]{0:T(1024)(128)(4,1)}), s8[4194304]{0:T(1024)(128)(4,1)S(1)}, s32[]{:S(2)}) async-start(s8[7340032]{0:T(1024)(128)(4,1)} %bitcast.58), calls=%async_computation.4 | async-start | bytes 8388608
  39.9 95.6 %slice-start.2 = ((s8[7340032]{0:T(1024)(128)(4,1)}), s8[4194304]{0:T(1024)(128)(4,1)S(1)}, s32[]{:S(2)}) async-start(s8[7340032]{0:T(1024)(128)(4,1)} %bitcast.60), calls=%async_computation.5 | async-start | bytes 8388608
  131.5 4.0 %slice-start.3 = ((s8[7340032]{0:T(1024)(128)(4,1)}), s8[3145728]{0:T(1024)(128)(4,1)S(1)}, s32[]{:S(2)}) async-start(s8[7340032]{0:T(1024)(128)(4,1)} %bitcast.60), calls=%async_computation.6 | async-start | bytes 6291456
  148.7 111.0 %all-to-all-start.1 = ((bf16[16,32,7168]{2,1,0:T(8,128)(2,1)}), bf16[16,32,7168]{2,1,0:T(8,128)(2,1)}, u32[]{:S(2)}, u32[]{:S(2)}) async-start(bf16[16,32,7168]{2,1,0:T(8,128)(2,1)} %bitcast.54), calls=%async_computation.1 | async-start | bytes 14680064 | tf_op jit(solution)/shard_map/all_to_all | solution.py:73
  265.6 4.8 %collective-permute-start.1 = (bf16[64,7168]{1,0:T(8,128)(2,1)S(1)}, bf16[64,7168]{1,0:T(8,128)(2,1)S(1)}, u32[]{:S(2)}, u32[]{:S(2)}) collective-permute-start(bf16[64,7168]{1,0:T(8,128)(2,1)S(1)} %slice.47), channel_id=1, source_target_pairs={{0,1},{1,0},{2,3},{3,2},{4,5},{5,4},{6,7},{7,6},{8,9},{9,8},{10,11... | collective-permute-start | bytes 2752520 | tf_op jit(solution)/shard_map/ppermute | solution.py:13
